TPU v7x, 128 devices: a whole 4x4x4 slice. The times are simulated.
128 devices in a mesh: src: 8 (over x, core), tgt: 16 (over y, z).
Axes of the slice: x: 4, y: 4, z: 4, core: 2. Of those that a mesh axis runs over, the one named last changes fastest.
Arguments:
- source_points: float32 [3, 524288], P(None, ('src', 'tgt')), may hold values from 0 to 2
- source_values: bfloat16 [524288, 128], P(('src', 'tgt')), may hold values from -0.031982422 to 0.033935547
- leaf_index: int32 [1024, 512], P(('src', 'tgt')), may hold values from 0 to 4095, as said below
- leaf_pivots: int32 [1024, 256], P(('src', 'tgt')), may hold values from 0 to 511, as said below
- leaf_proj: bfloat16 [1024, 256, 512], P(('src', 'tgt')), may hold values from -0.25 to 0.25
- node_pivots: int32 [128, 256], P(('src', 'tgt')), may hold values from 0 to 2047, as said below
- node_proj: bfloat16 [128, 256, 2048], P(('src', 'tgt')), may hold values from -0.125 to 0.125
- top_pivots: int32 [16, 256], P('tgt'), may hold values from 0 to 2047, as said below
- top_proj: bfloat16 [16, 256, 2048], P('tgt', None, 'src'), may hold values from -0.125 to 0.125
- target_points: float32 [3, 65536], P(None, 'tgt'), may hold values from 0 to 2
- near_list: int32 [8, 256, 8], P('src', 'tgt'), may hold values from 0 to 23, as said below
- near_count: int32 [8, 256], P('src', 'tgt'), may hold values from 0 to 8, as said below
- far_list: int32 [8, 256, 12], P('src', 'tgt'), may hold values from 0 to 23, as said below
- far_count: int32 [8, 256], P('src', 'tgt'), may hold values from 0 to 12, as said below
- node_list: int32 [8, 256, 4], P('src', 'tgt'), may hold values from 0 to 15, as said below
- node_count: int32 [8, 256], P('src', 'tgt'), may hold values from 0 to 4, as said below
- top_list: int32 [256, 12], P('tgt'), may hold values from 0 to 15, as said below
- top_count: int32 [256], P('tgt'), may hold values from 1 to 12, as said below
Outputs:
- posterior: float32 [65536, 128], P('tgt', 'src')
Inputs may be any that keep to these rules, and one draw needn't show every extreme that they name: `leaf_index`: each block of 8 rows (one node) holds every number of 0 to 4095 once. `leaf_pivots`: entries of a row are distinct. `node_pivots`: entries of a row are distinct. `top_pivots`: entries of a row are distinct. `near_list`: entries of a row are distinct and differ from those of far_list in the same row. `far_list`: entries of a row are distinct. `near_count`: zero for target leaves whose block differs from i by more than one; in each block and column some target leaf reaches 8. `far_count`: zero for target leaves whose block differs from i by more than one; in each block and column some target leaf reaches 12. `node_list`: entries of a row are distinct. `node_count`: zero for target leaves whose block differs from i by at most one; in each block and column some target leaf reaches 4. `top_list`: entries of a row are distinct. `top_count`: in each column some target leaf reaches 12.
All inputs are finite; a program needn't handle non-finite values.
Results may differ from a plain program's by a relative error of at most 0.0075.
Values may be sent and summed in bfloat16 or wider, within the bound.
No kernel may reach another device: no remote copies, remote signals or barrier semaphores. Data moves between devices by JAX's collectives and lax.ppermute only.
A program may use at most 64 MiB of HBM per device.

v0:
```python
import jax
import jax.numpy as jnp
from jax import lax
from jax.sharding import PartitionSpec as P

SL = 8
TLEAF = 256
TLX = 2


rate = 2.0


def padded(block, sides, width):
    for axis, dim in sides:
        count = lax.axis_size(axis)
        forward = [(i, i + 1) for i in range(count - 1)]
        backward = [(target, source) for source, target in forward]
        low = lax.ppermute(
            lax.slice_in_dim(block, block.shape[dim] - width, None, axis=dim), axis, forward
        )
        high = lax.ppermute(lax.slice_in_dim(block, 0, width, axis=dim), axis, backward)
        block = jnp.concatenate([low, block, high], axis=dim)
    return block


def matern(targets, points):
    diff = targets[..., :, :, None] - points[..., :, None, :]
    dist = jnp.sqrt(jnp.sum(diff * diff, axis=-3))
    scaled = rate * dist
    return (1.0 + scaled) * jnp.exp(-scaled)


def alive_mask(counts, breadth):
    return jnp.arange(breadth, dtype=jnp.int32)[None, :] < counts[:, None]


def padded_sums(targets, lists, alive, points, values):
    breadth = lists.shape[1]
    extent = points.shape[2]
    columns = values.shape[2]

    def single_tile(member):
        target_pts, picked, alive_row = member
        gathered_pts = jnp.transpose(points[picked], (1, 0, 2)).reshape(3, breadth * extent)
        gathered_vals = values[picked].reshape(breadth * extent, columns)
        kernel = matern(target_pts, gathered_pts)
        kernel = jnp.where(jnp.repeat(alive_row, extent)[None, :], kernel, 0.0).astype(jnp.bfloat16)
        return jnp.dot(kernel, gathered_vals, preferred_element_type=jnp.float32)

    return lax.map(single_tile, (targets, lists, alive))


def tile_sums(targets, lists, counts, points, values):
    alive = alive_mask(counts, lists.shape[1])
    return padded_sums(targets, lists, alive, points, values)


def shards(
    source_points,
    source_values,
    leaf_index,
    leaf_pivots,
    leaf_proj,
    node_pivots,
    node_proj,
    top_pivots,
    top_proj,
    target_points,
    near_list,
    near_count,
    far_list,
    far_count,
    node_list,
    node_count,
    top_list,
    top_count,
):
    columns = source_values.shape[1]
    leaves = leaf_index.shape[0]
    leaf_size = leaf_index.shape[1]
    skel_size = leaf_pivots.shape[1]
    leaf_vals = source_values[leaf_index]
    leaf_pts = jnp.transpose(source_points[:, leaf_index], (1, 0, 2))
    skel_pts = jnp.take_along_axis(
        leaf_pts, jnp.broadcast_to(leaf_pivots[:, None, :], (leaves, 3, skel_size)), axis=2
    )
    skel_vals = jnp.einsum(
        "lsm,lmq->lsq", leaf_proj, leaf_vals, preferred_element_type=jnp.float32
    ).astype(jnp.bfloat16)
    node_vals = jnp.dot(
        node_proj[0],
        skel_vals.reshape(leaves * skel_size, columns),
        preferred_element_type=jnp.float32,
    ).astype(jnp.bfloat16)
    child_pts = jnp.transpose(skel_pts, (1, 0, 2)).reshape(3, leaves * skel_size)
    node_pts = child_pts[:, node_pivots[0]]
    halo_vals = padded(jnp.concatenate([leaf_vals, skel_vals], axis=1), (("tgt", 0),), SL)
    halo_pts = padded(jnp.concatenate([leaf_pts, skel_pts], axis=2), (("tgt", 0),), SL)
    top_term = jnp.dot(top_proj[0], node_vals, preferred_element_type=jnp.float32)
    src_index = lax.axis_index("src")
    top_sum = lax.psum(top_term, "src")
    every_pts = lax.all_gather(node_pts, "src", axis=1, tiled=True)
    top_pts = every_pts[:, top_pivots[0]]
    top_vals = top_sum.astype(jnp.bfloat16)
    node_all_vals, node_all_pts = (
        lax.all_gather(node_vals[None], "tgt", axis=0, tiled=True),
        lax.all_gather(node_pts[None].astype(jnp.bfloat16), "tgt", axis=0, tiled=True).astype(
            jnp.float32
        ),
    )
    top_all_vals, top_all_pts = (
        lax.all_gather(top_vals[None], "tgt", axis=0, tiled=True),
        lax.all_gather(top_pts[None].astype(jnp.bfloat16), "tgt", axis=0, tiled=True).astype(
            jnp.float32
        ),
    )
    targets = jnp.transpose(target_points.reshape(3, -1, TLEAF), (1, 0, 2))
    near = tile_sums(
        targets, near_list[0], near_count[0], halo_pts[:, :, :leaf_size], halo_vals[:, :leaf_size]
    )
    far = tile_sums(
        targets, far_list[0], far_count[0], halo_pts[:, :, leaf_size:], halo_vals[:, leaf_size:]
    )
    nodes = tile_sums(targets, node_list[0], node_count[0], node_all_pts, node_all_vals)
    partial_value = near + far + nodes
    start = src_index * TLX
    top_rows = tile_sums(
        lax.dynamic_slice_in_dim(targets, start, TLX, 0),
        lax.dynamic_slice_in_dim(top_list, start, TLX, 0),
        lax.dynamic_slice_in_dim(top_count, start, TLX, 0),
        top_all_pts,
        top_all_vals,
    )
    current = lax.dynamic_slice_in_dim(partial_value, start, TLX, 0)
    partial_value = lax.dynamic_update_slice_in_dim(partial_value, current + top_rows, start, 0)
    flat_terms = partial_value.reshape(-1, columns)
    return lax.psum_scatter(flat_terms, "src", scatter_dimension=1, tiled=True)


def solution(mesh):
    in_specs = (
        P(None, ("src", "tgt")),
        P(("src", "tgt"), None),
        P(("src", "tgt"), None),
        P(("src", "tgt"), None),
        P(("src", "tgt"), None, None),
        P(("src", "tgt"), None),
        P(("src", "tgt"), None, None),
        P("tgt", None),
        P("tgt", None, "src"),
        P(None, "tgt"),
        P("src", "tgt", None),
        P("src", "tgt"),
        P("src", "tgt", None),
        P("src", "tgt"),
        P("src", "tgt", None),
        P("src", "tgt"),
        P("tgt", None),
        P("tgt"),
    )
    out_specs = P("tgt", "src")
    return jax.shard_map(shards, mesh=mesh, in_specs=in_specs, out_specs=out_specs, check_vma=False)
```

profile of v0, /device:TPU:8, one launch (start us, length us, event | category | flops | bytes accessed | tf_op | source)
XLA Modules:
  0.0 784.0 jit_solution(391232090339406623)
XLA Ops:
  7.4 12.4 %gather_fusion.9 = bf16[4096,128]{1,0:T(8,128)(2,1)S(1)} fusion(bf16[4096,128]{1,0:T(8,128)(2,1)} %param.27, s32[4096]{0:T(1024)S(1)} %broadcast_clamp_fusion), kind=kCustom, calls=%fused_computation.9 | custom fusion | bytes 2113536 | tf_op jit(solution)/shard_map/gather | solution.py:83
  28.2 15.7 %gather_fusion.8 = f32[4096,3]{1,0:T(8,128)} fusion(f32[3,4096]{0,1:T(8,128)} %copy.60, s32[4096]{0:T(1024)S(1)} %broadcast_clamp_fusion), kind=kCustom, calls=%fused_computation.8 | custom fusion | bytes 114688 | tf_op jit(solution)/shard_map/gather | solution.py:84
  46.2 60.2 %gather_fusion.12 = f32[6144]{0:T(1024)S(1)} fusion(f32[8,3,512]{2,1,0:T(4,128)S(1)} %bitcast.211, s32[6144]{0:T(1024)S(1)} %reshape.348), kind=kCustom, calls=%fused_computation.12 | custom fusion | bytes 122880 | tf_op jit(solution)/shard_map/jit(take_along_axis)/gather | solution.py:85
  119.5 6.0 collective-permute-start.3
  125.7 28.0 %all-reduce.1 = bf16[256,128]{0,1:T(8,128)(2,1)} all-reduce(f32[256,128]{0,1:T(8,128)S(1)} %convolution_bitcast_fusion.1), channel_id=1, replica_groups=mesh['src'=8,'tgt'=16] {'src'}, use_global_device_ids=true, to_apply=%region_9.10 | all-reduce | flops 32768 | bytes 196608 | tf_op jit(solution)/shard_map/psum | solution.py:102
  157.1 21.8 %all-gather.5 = bf16[16,3,256]{2,1,0:T(4,128)(2,1)S(1)} all-gather(bf16[1,3,256]{2,1,0:T(4,128)(2,1)S(1)} %copy.67), channel_id=2, replica_groups=mesh['src'=8,'tgt'=16] {'tgt'}, dimensions={0}, use_global_device_ids=true | all-gather | bytes 26112 | tf_op jit(solution)/shard_map/all_gather | solution.py:108
  179.6 14.2 %all-gather.2 = bf16[3,2048]{0,1:T(8,128)(2,1)} all-gather(bf16[3,256]{0,1:T(8,128)(2,1)S(1)} %bitcast.233), channel_id=4, replica_groups=mesh['src'=8,'tgt'=16] {'src'}, dimensions={1}, use_global_device_ids=true | all-gather | bytes 13824 | tf_op jit(solution)/shard_map/all_gather | solution.py:103
  195.7 22.6 %all-gather.6 = bf16[16,3,256]{2,1,0:T(4,128)(2,1)S(1)} all-gather(bf16[1,3,256]{2,1,0:T(4,128)(2,1)S(1)} %copy.71), channel_id=5, replica_groups=mesh['src'=8,'tgt'=16] {'tgt'}, dimensions={0}, use_global_device_ids=true | all-gather | bytes 26112 | tf_op jit(solution)/shard_map/all_gather | solution.py:114
  226.3 186.5 %while.41 = (s32[]{:T(128)}, f32[16,256,128]{2,1,0:T(8,128)}, pred[16,12]{1,0:T(8,128)(4,1)S(1)}, f32[16,3,256]{2,1,0:T(4,128)}, s32[16,12]{1,0:T(8,128)S(1)}, /...) while((s32[]{:T(128)}, f32[16,256,128]{2,1,0:T(8,128)}, ...), condition=%wide.region_5.6_spmd, body=%wide.region_3.5_spmd.sunk | while | flops 212337696 | bytes 8918901 | solution.py:51
  233.6 4.3 fusion.69
  245.2 4.3 fusion.69
  256.9 4.3 fusion.69
  268.5 4.3 fusion.69
  280.2 4.3 fusion.69
  291.8 4.3 fusion.69
  303.5 4.3 fusion.69
  315.2 4.3 fusion.69
  326.8 4.3 fusion.69
  338.5 4.3 fusion.69
  350.1 4.3 fusion.69
  361.8 4.3 fusion.69
  373.5 4.3 fusion.69
  385.1 4.3 fusion.69
  396.8 4.3 fusion.69
  408.4 4.3 fusion.69
  419.5 201.4 %while.40 = (s32[]{:T(128)}, f32[16,256,128]{2,1,0:T(8,128)}, pred[16,8]{1,0:T(8,128)(4,1)S(1)}, f32[16,3,256]{2,1,0:T(4,128)}, s32[16,8]{1,0:T(8,128)S(1)}, /*i...) while((s32[]{:T(128)}, f32[16,256,128]{2,1,0:T(8,128)}, pred[16,8]{1,0:T(8,128)(4,1)S(1)}, ...), condition=%wide.region_2.3_spmd, body=%wide.region_0.2_spmd.sunk | while | flops 283116576 | bytes 11843353 | solution.py:51
  427.2 4.9 fusion.66
  439.8 4.9 fusion.66
  452.3 4.9 fusion.66
  464.9 4.9 fusion.66
  477.5 4.9 fusion.66
  490.1 4.9 fusion.66
  502.7 4.9 fusion.66
  515.3 4.9 fusion.66
  527.9 4.9 fusion.66
  540.5 4.9 fusion.66
  553.1 4.9 fusion.66
  565.6 4.9 fusion.66
  578.2 4.9 fusion.66
  590.8 4.9 fusion.66
  603.4 4.9 fusion.66
  616.0 4.9 fusion.66
  624.8 91.0 %while.42 = (s32[]{:T(128)}, f32[16,256,128]{2,1,0:T(8,128)}, pred[16,4]{1,0:T(8,128)(4,1)S(1)}, f32[16,3,256]{2,1,0:T(4,128)}, s32[16,4]{1,0:T(8,128)S(1)}, /*i...) while((s32[]{:T(128)}, f32[16,256,128]{2,1,0:T(8,128)}, pred[16,4]{1,0:T(8,128)(4,1)S(1)}, ...), condition=%wide.region_8.9_spmd, body=%wide.region_6.8_spmd.sunk | while | flops 70779920 | bytes 3069629 | solution.py:51
  717.4 19.3 %while.43 = (s32[]{:T(128)}, f32[2,256,128]{2,1,0:T(8,128)}, pred[2,12]{1,0:T(4,128)(4,1)S(1)}, f32[2,3,256]{2,1,0:T(4,128)S(1)}, s32[2,12]{1,0:T(2,128)S(1)}, /...) while((s32[]{:T(128)}, f32[2,256,128]{2,1,0:T(8,128)}, ...), condition=%wide.region_12.13_spmd, body=%wide.region_10.12_spmd.sunk | while | flops 212337696 | bytes 8918901 | solution.py:51
  722.8 4.3 fusion.75
  732.3 4.3 fusion.75
  736.7 4.6 add_add_fusion
  745.9 31.6 %reduce-scatter.2.cloned.1.call-done = f32[4096,16]{0,1:T(8,128)} async-done(((f32[4096,128]{0,1:T(8,128)}), f32[4096,16]{0,1:T(8,128)}) %reduce-scatter.2.cloned.1.call-update) | async-done | bytes 262160 | tf_op jit(solution)/shard_map/reduce_scatter | solution.py:138
  (567 shorter events, 395.4 us)
Async XLA Ops:
  6.5 13.3 %copy-start = (bf16[8,256,512]{2,1,0:T(8,128)(2,1)S(1)}, bf16[8,256,512]{2,1,0:T(8,128)(2,1)}, u32[]{:S(2)}) copy-start(bf16[8,256,512]{2,1,0:T(8,128)(2,1)} %param.30) | copy-start | bytes 6291460
  6.5 614.4 %all-gather.10.cloned.1.call-start = ((), (), s32[]{:S(2)}) async-start(), calls=%async_computation.2 | async-start | bytes 1114112 | tf_op jit(solution)/shard_map/all_gather | solution.py:107
  19.8 6.3 copy-start.6
  23.6 22.6 %copy-start.4 = (s32[8,256]{1,0:T(8,128)S(1)}, s32[8,256]{1,0:T(8,128)}, u32[]{:S(2)}) copy-start(s32[8,256]{1,0:T(8,128)} %param.29) | copy-start | bytes 24580
  26.1 689.6 %all-gather.12.cloned.1.call-start = ((), (), s32[]{:S(2)}) async-start(), calls=%async_computation.3 | async-start | bytes 1114112 | tf_op jit(solution)/shard_map/all_gather | solution.py:113
  106.4 19.1 %copy-start.2 = (bf16[128,256]{1,0:T(8,128)(2,1)S(1)}, bf16[128,256]{1,0:T(8,128)(2,1)}, u32[]{:S(2)}) copy-start(bf16[128,256]{1,0:T(8,128)(2,1)} %convolution_convert_fusion.1) | copy-start | bytes 196612
  106.4 48.5 %copy-start.10 = (s32[1,256]{1,0:T(1,128)S(1)}, s32[1,256]{1,0:T(1,128)}, u32[]{:S(2)}) copy-start(s32[1,256]{1,0:T(1,128)} %param.33) | copy-start | bytes 3076
  106.4 48.5 %copy-start.11 = (s32[1,256]{1,0:T(1,128)S(1)}, s32[1,256]{1,0:T(1,128)}, u32[]{:S(2)}) copy-start(s32[1,256]{1,0:T(1,128)} %param.31) | copy-start | bytes 3076
  106.4 50.4 %copy-start.7 = (s32[1,16,12]{1,0,2:T(1,128)S(1)}, s32[1,16,12]{1,0,2:T(1,128)}, u32[]{:S(2)}) copy-start(s32[1,16,12]{1,0,2:T(1,128)} %param.38) | copy-start | bytes 2308
  106.5 50.5 %copy-start.8 = (s32[1,16,8]{1,2,0:T(8,128)S(1)}, s32[1,16,8]{1,2,0:T(8,128)}, u32[]{:S(2)}) copy-start(s32[1,16,8]{1,2,0:T(8,128)} %param.36) | copy-start | bytes 1540
  106.5 73.0 %copy-start.9 = (s32[1,16,4]{1,2,0:T(4,128)S(1)}, s32[1,16,4]{1,2,0:T(4,128)}, u32[]{:S(2)}) copy-start(s32[1,16,4]{1,2,0:T(4,128)} %param.40) | copy-start | bytes 772
  106.5 111.8 %copy-start.15 = (s32[16]{0:T(128)S(1)}, s32[16]{0:T(128)}, u32[]{:S(2)}) copy-start(s32[16]{0:T(128)} %param.43) | copy-start | bytes 196
  106.5 112.7 %copy-start.12 = (s32[1,16]{1,0:T(1,128)S(1)}, s32[1,16]{1,0:T(1,128)}, u32[]{:S(2)}) copy-start(s32[1,16]{1,0:T(1,128)} %param.39) | copy-start | bytes 196
  106.5 112.8 %copy-start.13 = (s32[1,16]{1,0:T(1,128)S(1)}, s32[1,16]{1,0:T(1,128)}, u32[]{:S(2)}) copy-start(s32[1,16]{1,0:T(1,128)} %param.37) | copy-start | bytes 196
  106.5 112.8 %copy-start.14 = (s32[1,16]{1,0:T(1,128)S(1)}, s32[1,16]{1,0:T(1,128)}, u32[]{:S(2)}) copy-start(s32[1,16]{1,0:T(1,128)} %param.41) | copy-start | bytes 196
  106.5 19.0 %copy-start.5 = (bf16[1,256,256]{2,1,0:T(8,128)(2,1)S(1)}, bf16[1,256,256]{2,1,0:T(8,128)(2,1)}, u32[]{:S(2)}) copy-start(bf16[1,256,256]{2,1,0:T(8,128)(2,1)} %param.34) | copy-start | bytes 393220
  107.3 112.9 %collective-permute-start = (f32[8,3,768]{2,1,0:T(4,128)}, f32[8,3,768]{2,1,0:T(4,128)}, u32[]{:S(2)}, u32[]{:S(2)}) collective-permute-start(f32[8,3,768]{2,1,0:T(4,128)} %pad_maximum_fusion.5), channel_id=1, source_target_pairs={{0,1},{1,2},{2,3},{3,4},{4,5},{5,6},{6,7},{7,8},{8,9},{9,10},{10,1... | collective-permute-start | bytes 221192 | tf_op jit(solution)/shard_map/ppermute | solution.py:19
  111.1 109.0 %collective-permute-start.1 = (f32[8,3,768]{2,1,0:T(4,128)}, f32[8,3,768]{2,1,0:T(4,128)}, u32[]{:S(2)}, u32[]{:S(2)}) collective-permute-start(f32[8,3,768]{2,1,0:T(4,128)} %pad_maximum_fusion.5), channel_id=1, source_target_pairs={{1,0},{2,1},{3,2},{4,3},{5,4},{6,5},{7,6},{8,7},{9,8},{10,9},{11,1... | collective-permute-start | bytes 221192 | tf_op jit(solution)/shard_map/ppermute | solution.py:22
  117.5 104.5 %collective-permute-start.2 = (bf16[8,768,128]{2,1,0:T(8,128)(2,1)}, bf16[8,768,128]{2,1,0:T(8,128)(2,1)}, u32[]{:S(2)}, u32[]{:S(2)}) collective-permute-start(bf16[8,768,128]{2,1,0:T(8,128)(2,1)} %pad_maximum_fusion.2), channel_id=1, source_target_pairs={{0,1},{1,2},{2,3},{3,4},{4,5},{5,6},{6,7},{7,8},{8,9},{9,10},{10,1... | collective-permute-start | bytes 4718600 | tf_op jit(solution)/shard_map/ppermute | solution.py:19
  119.5 102.6 %collective-permute-start.3 = (bf16[8,768,128]{2,1,0:T(8,128)(2,1)}, bf16[8,768,128]{2,1,0:T(8,128)(2,1)}, u32[]{:S(2)}, u32[]{:S(2)}) collective-permute-start(bf16[8,768,128]{2,1,0:T(8,128)(2,1)} %pad_maximum_fusion.2), channel_id=1, source_target_pairs={{1,0},{2,1},{3,2},{4,3},{5,4},{6,5},{7,6},{8,7},{9,8},{10,9},{11,1... | collective-permute-start | bytes 4718600 | tf_op jit(solution)/shard_map/ppermute | solution.py:22
  153.8 623.7 %reduce-scatter.2.cloned.1.call-start = ((), (), s32[]{:S(2)}) async-start(), calls=%async_computation.1 | async-start | bytes 2359296 | tf_op jit(solution)/shard_map/reduce_scatter | solution.py:138
  221.1 0.9 copy-start.1
  415.9 3.6 slice-start
  736.7 4.6 copy-start.3
Sparse Core Ops, SparseCore 0:
  26.2 45.4 all-gather.9
  153.9 39.6 all-gather.11
  746.0 31.3 reduce-scatter.1
where the time goes:
time: 790 us; the launch traced here: 784 us
  local copies, waits for them, and re-layouts  319 us (40%)
  matrix products  181 us (23%)
  other arithmetic  135 us (17%)
  blocking collectives  86.6 us (11%)
  waiting for transfers between devices  31.6 us (4%)
  starting transfers between devices  16 us (2%)
  between operations  13.5 us (2%)
    dot_general x50, matrix products, single_tile(): return jnp.dot(kernel, gathered_vals, preferred_element_type=jnp.float32)  177 us
    gather x50, local copies, waits for them, and re-layouts, single_tile(): gathered_vals = values[picked].reshape(breadth * extent, columns)  123 us
    reduce_sum x50, other arithmetic, matern(): dist = jnp.sqrt(jnp.sum(diff * diff, axis=-3))  115 us
    gather x3, local copies, waits for them, and re-layouts, shards(): jnp.take_along_axis(leaf_pts, jnp.broadcast_to(leaf_pivots[:, None, :], (...  60.2 us
    gather x50, local copies, waits for them, and re-layouts, single_tile(): points[picked]  42.4 us
    sub x50, local copies, waits for them, and re-layouts, matern(): diff = targets[..., :, :, None] - points[..., :, None, :]  33.3 us
    reduce_scatter x1, waiting for transfers between devices, shards(): return lax.psum_scatter(flat_terms, 'src', scatter_dimension=1, tiled=True)  31.6 us
    psum x1, blocking collectives, shards(): top_sum = lax.psum(top_term, 'src')  28 us
  transfers between devices with their start and end apart: 7, of which 1 were waited for; matrix products, arithmetic and copies ran while one was open for 75% of the time, Pallas kernels for 0%

commit v1 on v0

v1 whole, which is shorter than its diff:
```python
import functools

import jax
import jax.numpy as jnp
from jax import lax
from jax.experimental import pallas as pl
from jax.experimental.pallas import tpu as pltpu
from jax.sharding import PartitionSpec as P

SL = 8
LEAF = 512
SKEL = 256
Q = 128
TLEAF = 256
TL_J = 16
WIN = 6
KF = 16
LN2 = 0.6931471805599453
SCALE = 2.0 / LN2
GROUP = 16
VMEM = pltpu.VMEM
SMEM = pltpu.SMEM
bf16 = jnp.bfloat16
f32 = jnp.float32
NEAR_AT, FAR_AT, NODE_AT, TOP_AT = 0, 8, 20, 24
NEAR_N, FAR_N, NODE_N, TOP_N = 36, 37, 38, 39
TRASH = 16


def split2(x):
    high = x.astype(bf16).astype(f32)
    return high, (x - high).astype(bf16).astype(f32)


def split3(x):
    high, rest = split2(x)
    return high, rest, (x - high - rest).astype(bf16).astype(f32)


def centred(x):
    return (x - 1.0) * SCALE


def features(coords, is_source):
    pieces = [split2(c) for c in coords]
    high = [p[0] for p in pieces]
    low = [p[1] for p in pieces]
    norm = sum((h + r) * (h + r) for h, r in pieces)
    norms = list(split3(norm))
    one = jnp.ones_like(norm)
    zero = jnp.zeros_like(norm)
    if is_source:
        high = [-2.0 * h for h in high]
        low = [-2.0 * r for r in low]
        return high + low + high + [one, one, one] + norms + [zero]
    return high + high + low + norms + [one, one, one] + [zero]


def matern(w):
    w = jnp.maximum(w, 1e-12)
    u = w * lax.rsqrt(w)
    return ((1.0 + LN2 * u) * jnp.exp2(-u)).astype(bf16)


def take(row, index):
    return jnp.take_along_axis(row, index, axis=1, mode="promise_in_bounds")


def pick(chunks, index):
    low = index & 127
    high = index >> 7
    result = jnp.zeros((8, 128), f32)
    for k, chunk in enumerate(chunks):
        result = jnp.where(high == k, take(chunk, low), result)
    return result


def lanes(x, m):
    return x[:, 128 * m : 128 * (m + 1)]


def leaf_kernel(
    meta, idx_s, idx, piv, npiv, tpiv, pts, vals, proj, nproj, tproj,
    v_out, f_out, n_out, t_out, wide, gathered, fs, ns,
):
    src, chip, core = meta[0], meta[1], meta[2]
    rows = vals.shape[0]

    def widen(k, _):
        at = pl.multiple_of(k * 512, 512)
        wide[pl.ds(at, 512), :] = vals[pl.ds(at, 512), :].astype(f32)
        return 0

    lax.fori_loop(0, rows // 512, widen, 0)

    def gather(k, _):
        leaf = k // 16
        base = (k % 16) * 32
        at = pl.multiple_of(k * 32, 32)
        for r in range(32):
            gathered[pl.ds(at + r, 1), :] = wide[pl.ds(idx_s[leaf, base + r], 1), :]
        return 0

    lax.fori_loop(0, rows // 32, gather, 0)

    for leaf in range(SL):
        leaf_vals = gathered[leaf * LEAF : (leaf + 1) * LEAF, :].astype(bf16)
        v_out[2 * leaf] = leaf_vals[:256]
        v_out[2 * leaf + 1] = leaf_vals[256:]
        v_out[16 + leaf] = jnp.dot(proj[leaf], leaf_vals, preferred_element_type=f32).astype(bf16)
    node_vals = jnp.dot(
        nproj[0], v_out[16:24].reshape(SL * SKEL, Q), preferred_element_type=f32
    ).astype(bf16)
    n_out[0:256, :] = node_vals
    top = jnp.dot(tproj[0], node_vals, preferred_element_type=f32).T

    index = idx[...]
    pivots = piv[...]
    node_piv = jnp.broadcast_to(npiv[...], (8, SKEL))
    top_piv = jnp.broadcast_to(tpiv[...], (8, SKEL))
    leaf_of = lax.broadcasted_iota(jnp.int32, (8, 128), 0)
    leaf_c, skel_c, node_c, top_c = [], [], [], []
    for c in range(3):
        chunks = [jnp.broadcast_to(pts[c : c + 1, 128 * k : 128 * (k + 1)], (8, 128)) for k in range(rows // 128)]
        leaf_x = [pick(chunks, lanes(index, m)) for m in range(4)]
        skel_x = [pick(leaf_x, lanes(pivots, m)) for m in range(2)]
        node_x = []
        top_x = []
        for m in range(2):
            at = lanes(node_piv, m)
            mine = jnp.where(leaf_of == (at >> 8), pick(skel_x, at & 255), 0.0)
            node_x.append(jnp.broadcast_to(jnp.sum(mine, axis=0, keepdims=True), (8, 128)))
        for m in range(2):
            at = lanes(top_piv, m)
            top_x.append(jnp.where((at >> 8) == src, centred(pick(node_x, at & 255)), 0.0))
        leaf_c.append(centred(jnp.concatenate(leaf_x, axis=1)))
        skel_c.append(centred(jnp.concatenate(skel_x, axis=1)))
        node_c.append(centred(jnp.concatenate(node_x, axis=1)))
        top_c.append(jnp.concatenate(top_x, axis=1))
    for f, (a, b, n) in enumerate(zip(features(leaf_c, True), features(skel_c, True), features(node_c, True))):
        for leaf in range(SL):
            fs[2 * leaf, f : f + 1, :] = a[leaf : leaf + 1, :256]
            fs[2 * leaf + 1, f : f + 1, :] = a[leaf : leaf + 1, 256:]
            fs[16 + leaf, f : f + 1, :] = b[leaf : leaf + 1, :]
        ns[f : f + 1, :] = n[0:1, :]
    f_out[...] = fs[...].astype(bf16)
    n_out[256:272, :] = ns[:, :128].astype(bf16)
    n_out[272:288, :] = ns[:, 128:].astype(bf16)
    ns[...] = jnp.zeros_like(ns)
    for c in range(3):
        for k, piece in enumerate(split3(top_c[c])):
            ns[3 * c + k : 3 * c + k + 1, :] = piece[0:1, :]
    pieces = ns[...].astype(bf16)
    for half in range(2):
        for x in range(4):
            for k in range(2):
                part = top[16 * (2 * x + k) : 16 * (2 * x + k) + 16, 128 * half : 128 * half + 128]
                at = (k ^ core, (x - chip) & 3)
                t_out[at[0], at[1], 32 * half : 32 * half + 16, :] = part.astype(bf16)
                t_out[at[0], at[1], 32 * half + 16 : 32 * half + 32, :] = lanes(pieces, half)


def target_rows(pts, fa):
    rows = features([centred(pts[c : c + 1, :]) for c in range(3)], False)
    for f, row in enumerate(rows):
        fa[f : f + 1, :] = row


def pad_pairs(ps, pt, n, trash):
    for r in range(GROUP):
        ps[n + r] = 0
        pt[n + r] = trash
    return (n + GROUP - 1) // GROUP


def run_pairs(ps, pt, turns, a_ref, f_ref, v_ref, acc):
    def step(g, _):
        for q in range(GROUP):
            s = ps[g * GROUP + q]
            t = pt[g * GROUP + q]
            w = jnp.dot(a_ref[t], f_ref[s], preferred_element_type=f32)
            acc[t] += jnp.dot(matern(w), v_ref[s], preferred_element_type=f32)
        return 0

    lax.fori_loop(0, turns, step, 0)


def leaf_pairs(ps, pt, n, lists, start, slot, base):
    def target(t, n):
        leaf = start + t

        def near(e, n):
            v = lists[leaf, NEAR_AT + e] - base
            ps[n] = 2 * v
            pt[n] = slot + t
            ps[n + 1] = 2 * v + 1
            pt[n + 1] = slot + t
            return n + jnp.where((v >= 0) & (v < SL), 2, 0)

        def far(e, n):
            v = lists[leaf, FAR_AT + e] - base
            ps[n] = 16 + v
            pt[n] = slot + t
            return n + jnp.where((v >= 0) & (v < SL), 1, 0)

        n = lax.fori_loop(0, lists[leaf, NEAR_N], near, n)
        return lax.fori_loop(0, lists[leaf, FAR_N], far, n)

    return lax.fori_loop(0, WIN, target, n)


def set_targets(fa, a_ref, start, slot):
    def one(t, _):
        at = pl.multiple_of((start + t) * TLEAF, TLEAF)
        a_ref[slot + t] = fa[:, pl.ds(at, TLEAF)].T.astype(bf16)
        return 0

    return one


def clear(acc):
    def one(t, _):
        acc[t] = jnp.zeros(acc.shape[1:], f32)
        return 0

    lax.fori_loop(0, acc.shape[0], one, 0)


def halo_kernel(meta, lists_l, lists_r, pts_l, pts_r, v_ref, f_ref, out_l, out_r, fa, a_ref, acc, ps, pt):
    start = meta[6]
    clear(acc)
    target_rows(pts_l, fa)
    lax.fori_loop(0, WIN, set_targets(fa, a_ref, start, 0), 0)
    target_rows(pts_r, fa)
    lax.fori_loop(0, WIN, set_targets(fa, a_ref, start, WIN), 0)
    a_ref[2 * WIN] = jnp.zeros((TLEAF, KF), bf16)
    n = leaf_pairs(ps, pt, 0, lists_l, start, 0, 16)
    n = leaf_pairs(ps, pt, n, lists_r, start, WIN, 0)
    run_pairs(ps, pt, pad_pairs(ps, pt, n, 2 * WIN), a_ref, f_ref, v_ref, acc)
    for t in range(WIN):
        out_l[t * TLEAF : (t + 1) * TLEAF, :] = acc[t].astype(bf16)
        out_r[t * TLEAF : (t + 1) * TLEAF, :] = acc[WIN + t].astype(bf16)


def own_kernel(meta, lists, pts, v_ref, f_ref, out, fa, a_ref, acc, ps, pt):
    start = meta[6]
    clear(acc)
    target_rows(pts, fa)
    lax.fori_loop(0, WIN, set_targets(fa, a_ref, start, 0), 0)
    a_ref[WIN] = jnp.zeros((TLEAF, KF), bf16)
    n = leaf_pairs(ps, pt, 0, lists, start, 0, 8)
    run_pairs(ps, pt, pad_pairs(ps, pt, n, WIN), a_ref, f_ref, v_ref, acc)
    for t in range(WIN):
        out[t] = acc[t]


def listed_pairs(ps, pt, lists, first, count_at, row, plane):
    def target(t, n):
        def one(e, n):
            column = lists[t, first + e]
            dr = (row - (column >> 2)) & 3
            dp = (plane - (column & 3)) & 3
            ps[n] = 4 * dr + dp
            pt[n] = t
            return n + 1

        return lax.fori_loop(0, lists[t, count_at], one, n)

    return lax.fori_loop(0, TL_J, target, 0)


def node_kernel(
    meta, lists, pts, own, halo_l, halo_r, y0, y1, y2, y3,
    out, fa, a_ref, acc, ys, f_ref, v_ref, ps, pt, sems,
):
    core, chip, row, plane, start = meta[2], meta[1], meta[4], meta[5], meta[6]
    copies = [pltpu.make_async_copy(y, ys.at[k], sems.at[k]) for k, y in enumerate((y0, y1, y2, y3))]
    for copy in copies:
        copy.start()
    clear(acc)
    for t in range(WIN):
        sides = halo_l[t * TLEAF : (t + 1) * TLEAF, :].astype(f32) + halo_r[t * TLEAF : (t + 1) * TLEAF, :].astype(f32)
        acc[start + t] = own[t] + sides
    target_rows(pts, fa)
    lax.fori_loop(0, TL_J, set_targets(fa, a_ref, 0, 0), 0)
    a_ref[TRASH] = jnp.zeros((TLEAF, KF), bf16)
    n = listed_pairs(ps, pt, lists, NODE_AT, NODE_N, row, plane)
    turns = pad_pairs(ps, pt, n, TRASH)
    for copy in copies:
        copy.wait()
    for k in range(4):
        for z in range(4):
            v_ref[4 * k + z] = ys[k, z * 288 : z * 288 + 256, :]
            f_ref[4 * k + z, :, 0:128] = ys[k, z * 288 + 256 : z * 288 + 272, :]
            f_ref[4 * k + z, :, 128:256] = ys[k, z * 288 + 272 : z * 288 + 288, :]
    run_pairs(ps, pt, turns, a_ref, f_ref, v_ref, acc)

    def turn(t, _):
        at = pl.multiple_of(t * TLEAF, TLEAF)
        block = acc[t].T.astype(bf16)
        for x in range(4):
            for k in range(2):
                begin = 16 * (2 * x + k)
                out[k ^ core, (x - chip) & 3, :, pl.ds(at, TLEAF)] = block[begin : begin + 16]
        return 0

    lax.fori_loop(0, TL_J, turn, 0)


def top_kernel(meta, lists, pts, tops, out, fa, a_ref, acc, f_ref, v_ref, fw, ps, pt):
    row, plane = meta[4], meta[5]
    clear(acc)
    target_rows(pts, fa)
    lax.fori_loop(0, TL_J, set_targets(fa, a_ref, 0, 0), 0)
    a_ref[TRASH] = jnp.zeros((TLEAF, KF), bf16)
    n = listed_pairs(ps, pt, lists, TOP_AT, TOP_N, row, plane)
    turns = pad_pairs(ps, pt, n, TRASH)
    for dz in range(4):
        for dy in range(4):
            slot = 4 * dy + dz
            base = (dz * 4 + dy) * 64
            for half in range(2):
                at = base + 32 * half
                vals = tops[at : at + 16, :].astype(f32)
                v_ref[slot, 128 * half : 128 * half + 128, :] = vals.T.astype(bf16)
                pieces = tops[at + 16 : at + 32, :].astype(f32)
                coords = [
                    pieces[3 * c : 3 * c + 1] + pieces[3 * c + 1 : 3 * c + 2] + pieces[3 * c + 2 : 3 * c + 3]
                    for c in range(3)
                ]
                for f, line in enumerate(features(coords, True)):
                    fw[f : f + 1, 128 * half : 128 * half + 128] = line
            f_ref[slot] = fw[...].astype(bf16)
    run_pairs(ps, pt, turns, a_ref, f_ref, v_ref, acc)

    def turn(t, _):
        at = pl.multiple_of(t * TLEAF, TLEAF)
        out[:, pl.ds(at, TLEAF)] = acc[t].T
        return 0

    lax.fori_loop(0, TL_J, turn, 0)


def whole(count):
    return [pl.BlockSpec(memory_space=VMEM)] * count


def params(mebibytes):
    return pltpu.CompilerParams(vmem_limit_bytes=mebibytes << 20)


def cost(flops, moved):
    return pl.CostEstimate(flops=int(flops), bytes_accessed=int(moved), transcendentals=0)


def pair_scratch():
    return [pltpu.SMEM((512,), jnp.int32), pltpu.SMEM((512,), jnp.int32)]


def shift(axis, count, fn):
    return [(i, fn(i)) for i in range(count) if 0 <= fn(i) < count]


def shards(
    source_points, source_values, leaf_index, leaf_pivots, leaf_proj, node_pivots, node_proj,
    top_pivots, top_proj, target_points, near_list, near_count, far_list, far_count,
    node_list, node_count, top_list, top_count,
):
    src = lax.axis_index("src")
    tgt = lax.axis_index("tgt")
    start = jnp.clip(2 * src - 2, 0, TL_J - WIN)
    meta = jnp.stack([src, src // 2, src % 2, tgt, tgt // 4, tgt % 4, start, src * 0]).astype(jnp.int32)
    lists = jnp.concatenate(
        [near_list[0], far_list[0], node_list[0], top_list, near_count[0][:, None], far_count[0][:, None],
         node_count[0][:, None], top_count[:, None]], axis=1)
    forward = shift("tgt", 16, lambda i: i + 1)
    backward = shift("tgt", 16, lambda i: i - 1)
    pts_l = lax.ppermute(target_points, "tgt", forward)
    pts_r = lax.ppermute(target_points, "tgt", backward)
    lists_l = lax.ppermute(lists, "tgt", forward)
    lists_r = lax.ppermute(lists, "tgt", backward)

    smem = pl.BlockSpec(memory_space=SMEM)
    v_all, f_all, node_own, top_own = pl.pallas_call(
        leaf_kernel,
        out_shape=(
            jax.ShapeDtypeStruct((24, 256, Q), bf16),
            jax.ShapeDtypeStruct((24, KF, 256), bf16),
            jax.ShapeDtypeStruct((288, Q), bf16),
            jax.ShapeDtypeStruct((2, 4, 64, 128), bf16),
        ),
        in_specs=[smem, smem] + whole(9),
        out_specs=tuple(whole(4)),
        scratch_shapes=[
            VMEM((4096, Q), f32),
            VMEM((4096, Q), f32),
            VMEM((24, KF, 256), f32),
            VMEM((KF, 256), f32),
        ],
        compiler_params=params(40),
        cost_estimate=cost(2 * 8e6, 8e6),
        name="leaf_stage",
    )(meta, leaf_index, leaf_index, leaf_pivots, node_pivots, top_pivots, source_points, source_values,
      leaf_proj, node_proj, top_proj)

    zshift = [shift("tgt", 16, lambda i, d=d: (i // 4) * 4 + (i % 4 + d) % 4) for d in range(4)]
    yshift = [shift("tgt", 16, lambda i, d=d: ((i // 4 + d) % 4) * 4 + i % 4) for d in range(4)]
    xshift = [shift("src", 8, lambda i, d=d: (i + 2 * d) % 8) for d in range(4)]
    cores = shift("src", 8, lambda i: i ^ 1)

    top_pair = top_own[0] + lax.ppermute(top_own[1], "src", cores)
    node_z = [node_own] + [lax.ppermute(node_own, "tgt", zshift[d]) for d in (1, 2, 3)]
    top_sum = top_pair[0].astype(f32)
    for d in (1, 2, 3):
        top_sum = top_sum + lax.ppermute(top_pair[d], "src", xshift[d]).astype(f32)
    top_sum = top_sum.astype(bf16)

    halo_l, halo_r = pl.pallas_call(
        halo_kernel,
        out_shape=(jax.ShapeDtypeStruct((WIN * TLEAF, Q), bf16),) * 2,
        in_specs=[smem, smem, smem] + whole(4),
        out_specs=tuple(whole(2)),
        scratch_shapes=[
            VMEM((KF, TL_J * TLEAF), f32),
            VMEM((2 * WIN + 1, TLEAF, KF), bf16),
            VMEM((2 * WIN + 1, TLEAF, Q), f32),
        ] + pair_scratch(),
        compiler_params=params(40),
        cost_estimate=cost(9e9, 3e6),
        name="halo_terms",
    )(meta, lists_l, lists_r, pts_l, pts_r, v_all, f_all)
    got_r = lax.ppermute(halo_l, "tgt", backward)
    got_l = lax.ppermute(halo_r, "tgt", forward)

    bundle = jnp.concatenate(node_z + [top_sum], axis=0)
    ys = [bundle] + [lax.ppermute(bundle, "tgt", yshift[d]) for d in (1, 2, 3)]
    top_y = jnp.concatenate([y[4 * 288 :] for y in ys], axis=0)
    tops = jnp.concatenate([top_y] + [lax.ppermute(top_y, "tgt", zshift[d]) for d in (1, 2, 3)], axis=0)

    own = pl.pallas_call(
        own_kernel,
        out_shape=jax.ShapeDtypeStruct((WIN, TLEAF, Q), f32),
        in_specs=[smem, smem] + whole(3),
        out_specs=pl.BlockSpec(memory_space=VMEM),
        scratch_shapes=[
            VMEM((KF, TL_J * TLEAF), f32),
            VMEM((WIN + 1, TLEAF, KF), bf16),
            VMEM((WIN + 1, TLEAF, Q), f32),
        ] + pair_scratch(),
        compiler_params=params(40),
        cost_estimate=cost(5e9, 3e6),
        name="own_terms",
    )(meta, lists, target_points, v_all, f_all)

    partial = pl.pallas_call(
        node_kernel,
        out_shape=jax.ShapeDtypeStruct((2, 4, 16, TL_J * TLEAF), bf16),
        in_specs=[smem, smem] + whole(4) + [pl.BlockSpec(memory_space=pl.ANY)] * 4,
        out_specs=pl.BlockSpec(memory_space=VMEM),
        scratch_shapes=[
            VMEM((KF, TL_J * TLEAF), f32),
            VMEM((TL_J + 1, TLEAF, KF), bf16),
            VMEM((TL_J + 1, TLEAF, Q), f32),
            VMEM((4, 4 * 288 + 64, Q), bf16),
            VMEM((16, KF, 256), bf16),
            VMEM((16, 256, Q), bf16),
        ] + pair_scratch() + [pltpu.SemaphoreType.DMA((4,))],
        compiler_params=params(40),
        cost_estimate=cost(4e9, 3e6),
        name="node_terms",
    )(meta, lists, target_points, own, got_l, got_r, *ys)

    top_term = pl.pallas_call(
        top_kernel,
        out_shape=jax.ShapeDtypeStruct((16, TL_J * TLEAF), f32),
        in_specs=[smem, smem] + whole(2),
        out_specs=pl.BlockSpec(memory_space=VMEM),
        scratch_shapes=[
            VMEM((KF, TL_J * TLEAF), f32),
            VMEM((TL_J + 1, TLEAF, KF), bf16),
            VMEM((TL_J + 1, TLEAF, 16), f32),
            VMEM((16, KF, 256), bf16),
            VMEM((16, 256, 16), bf16),
            VMEM((KF, 256), f32),
        ] + pair_scratch(),
        compiler_params=params(40),
        cost_estimate=cost(8e9, 3e6),
        name="top_terms",
    )(meta, lists, target_points, tops)

    pair = partial[0].astype(f32) + lax.ppermute(partial[1], "src", cores).astype(f32)
    total = pair[0] + top_term
    for d in (1, 2, 3):
        total = total + lax.ppermute(pair[d].astype(bf16), "src", xshift[d]).astype(f32)
    return total.T


def solution(mesh):
    both = ("src", "tgt")
    in_specs = (
        P(None, both), P(both, None), P(both, None), P(both, None), P(both, None, None), P(both, None),
        P(both, None, None), P("tgt", None), P("tgt", None, "src"), P(None, "tgt"), P("src", "tgt", None),
        P("src", "tgt"), P("src", "tgt", None), P("src", "tgt"), P("src", "tgt", None), P("src", "tgt"),
        P("tgt", None), P("tgt"),
    )
    return jax.shard_map(shards, mesh=mesh, in_specs=in_specs, out_specs=P("tgt", "src"), check_vma=False)
```

time: 790 us -> 152 us (0.19)
  local copies, waits for them, and re-layouts: 319 us -> 14.8 us
  matrix products: 181 us -> 0 us
  other arithmetic: 135 us -> 0.95 us
  blocking collectives: 86.6 us -> 0 us
  Pallas kernels: 0 us -> 61.5 us
  starting transfers between devices: 16 us -> 48.7 us
  between operations: 13.5 us -> 0.37 us
    gather x108 -> x0, local copies, waits for them, and re-layouts: 260 us -> none  [the longest x50 123 us: single_tile(): gathered_vals = values[picked].reshape(breadth * extent, columns)]
    dot_general x53 -> x0, matrix products: 181 us -> none  [the longest x50 177 us: single_tile(): return jnp.dot(kernel, gathered_vals, preferred_element_type=jnp.float32)]
    reduce_sum x50 -> x0, other arithmetic: 115 us -> none  [matern(): dist = jnp.sqrt(jnp.sum(diff * diff, axis=-3))]
    pallas_call x0 -> x5, Pallas kernels: none -> 61.5 us  [the longest x1 19.8 us: shards(): pl.pallas_call(top_kernel, out_shape=jax.ShapeDtypeStruct((16, TL_J * TLE...]
    all_gather x3 -> x0, blocking collectives: 58.6 us -> none  [the longest x1 22.6 us: shards(): lax.all_gather(top_pts[None].astype(jnp.bfloat16), 'tgt', axis=0, tiled=T...]
    sub x50 -> x0, local copies, waits for them, and re-layouts: 33.3 us -> none  [matern(): diff = targets[..., :, :, None] - points[..., :, None, :]]
    ppermute x4 -> x23, starting transfers between devices: 15.9 us -> 48.7 us  [the longest x3 6.8 us: shards(): top_sum = top_sum + lax.ppermute(top_pair[d], 'src', xshift[d]).astype(f32)]
    reduce_scatter x1 -> x0, waiting for transfers between devices: 31.6 us -> none  [shards(): return lax.psum_scatter(flat_terms, 'src', scatter_dimension=1, tiled=True)]
  transfers between devices with their start and end apart: 7 -> 23, of which waited for: 1 -> 4; matrix products, arithmetic and copies ran while one was open for 75% -> 0% of each run, Pallas kernels for 0% -> 33%
where the time goes in v1:
time: 152 us
  Pallas kernels  61.5 us (40%)
  starting transfers between devices  48.7 us (32%)
  waiting for transfers between devices  25.3 us (17%)
  local copies, waits for them, and re-layouts  14.8 us (10%)
    ppermute x3, waiting for transfers between devices, shards(): ys = [bundle] + [lax.ppermute(bundle, 'tgt', yshift[d]) for d in (1, 2, 3)]  20.9 us
    pallas_call x1, Pallas kernels, shards(): pl.pallas_call(top_kernel, out_shape=jax.ShapeDtypeStruct((16, TL_J * TLE...  19.8 us
    pallas_call x1, Pallas kernels, shards(): pl.pallas_call(leaf_kernel, out_shape=(jax.ShapeDtypeStruct((24, 256, Q),...  13.7 us
    pallas_call x1, Pallas kernels, shards(): pl.pallas_call(halo_kernel, out_shape=(jax.ShapeDtypeStruct((WIN * TLEAF,...  11.1 us
    pallas_call x1, Pallas kernels, shards(): pl.pallas_call(node_kernel, out_shape=jax.ShapeDtypeStruct((2, 4, 16, TL_...  11 us
    unnamed x28, local copies, waits for them, and re-layouts  9.4 us
    ppermute x3, starting transfers between devices, shards(): top_sum = top_sum + lax.ppermute(top_pair[d], 'src', xshift[d]).astype(f32)  6.8 us
    ppermute x3, starting transfers between devices, shards(): ys = [bundle] + [lax.ppermute(bundle, 'tgt', yshift[d]) for d in (1, 2, 3)]  6.74 us
  transfers between devices with their start and end apart: 23, of which 4 were waited for; matrix products, arithmetic and copies ran while one was open for 0% of the time, Pallas kernels for 33%

profile of v1, /device:TPU:8, one launch (start us, length us, event | category | flops | bytes accessed | tf_op | source)
XLA Modules:
  0.0 151.8 jit_solution(11718423993334183056)
XLA Ops:
  0.0 0.8 copy.19
  0.8 0.8 copy.20
  1.5 0.8 copy.21
  2.3 0.7 copy.22
  3.0 0.7 copy.23
  3.7 0.7 copy.24
  4.5 0.7 copy.25
  5.2 0.8 concatenate.13.lists
  6.0 3.8 %collective-permute-start = (s32[16,40]{1,0:T(8,128)S(1)}, s32[16,40]{1,0:T(8,128)S(1)}, u32[]{:S(2)}, u32[]{:S(2)}) collective-permute-start(s32[16,40]{1,0:T(8,128)S(1)} %concatenate.13.lists), channel_id=1, source_target_pairs={{0,1},{1,2},{2,3},{3,4},{4,5},{5,6},{6,7},{7,8},{8,9},{9,10},{10,1... | collective-permute-start | bytes 7688 | tf_op jit(solution)/shard_map/ppermute | solution.py:380
  9.8 4.1 %collective-permute-start.1 = (s32[16,40]{1,0:T(8,128)S(1)}, s32[16,40]{1,0:T(8,128)S(1)}, u32[]{:S(2)}, u32[]{:S(2)}) collective-permute-start(s32[16,40]{1,0:T(8,128)S(1)} %concatenate.13.lists), channel_id=1, source_target_pairs={{1,0},{2,1},{3,2},{4,3},{5,4},{6,5},{7,6},{8,7},{9,8},{10,9},{11,1... | collective-permute-start | bytes 7688 | tf_op jit(solution)/shard_map/ppermute | solution.py:381
  14.0 0.1 stack.31.meta
  14.1 1.6 %copy-done = bf16[8,256,512]{2,1,0:T(8,128)(2,1)S(1)} copy-done((bf16[8,256,512]{2,1,0:T(8,128)(2,1)S(1)}, bf16[8,256,512]{2,1,0:T(8,128)(2,1)}, u32[]{:S(2)}) %copy-start) | copy-done | bytes 2097176
  15.7 1.2 copy-done.1
  16.9 1.2 copy-done.2
  18.1 0.9 copy-done.3
  19.0 0.8 copy-done.4
  19.9 0.7 copy-done.5
  20.6 0.7 copy-done.6
  21.3 0.7 copy-done.7
  22.0 0.7 copy-done.8
  22.7 13.7 %leaf_stage.1 = (bf16[24,256,128]{2,1,0:T(8,128)(2,1)S(1)}, bf16[24,16,256]{2,1,0:T(8,128)(2,1)S(1)}, bf16[288,128]{1,0:T(8,128)(2,1)S(1)}, bf16[2,4,64,128]{3,2,1,0:T(8,128)(2,1)S(1)}) custom-call(s32[8]{0:T(128)S(1)} %stack.31.meta, s32[8,512]{1,0:T(8,128)S(1)} %copy-done.5, s32[8,512]{1,0:T(8,128)S(1)} %copy-done.5, s32[8,256]{1,0:T(8,128)S(1)} %copy-done.6, ...), custom_call_target="tpu_custom_call" | custom-call | flops 16000000 | bytes 8000000 | tf_op jit(solution)/shard_map/leaf_stage/pallas_call | solution.py:384
  36.4 3.4 %collective-permute-start.7 = (bf16[288,128]{1,0:T(8,128)(2,1)S(1)}, bf16[288,128]{1,0:T(8,128)(2,1)S(1)}, u32[]{:S(2)}, u32[]{:S(2)}) collective-permute-start(bf16[288,128]{1,0:T(8,128)(2,1)S(1)} %get-tuple-element.15), channel_id=1, source_target_pairs={{0,2},{1,3},{2,0},{3,1},{4,6},{5,7},{6,4},{7,5},{8,10},{9,11},{10,... | collective-permute-start | bytes 221192 | tf_op jit(solution)/shard_map/ppermute | solution.py:412
  39.8 6.0 %own_terms.1.own = f32[6,256,128]{2,1,0:T(8,128)S(1)} custom-call(s32[8]{0:T(128)S(1)} %stack.31.meta, s32[16,40]{1,0:T(8,128)S(1)} %concatenate.13.lists, f32[3,4096]{1,0:T(4,128)S(1)} %copy-done.9, bf16[24,256,128]{2,1,0:T(8,128)(2,1)S(1)} %get-tuple-element.11.v_ref, bf16[24,16,256]{2,1,0:T(8,128)(2,1)S(1)} %get-tuple-element.12.f_ref), custom_call_target="tpu_custom_call" | custom-call | flops 5000000000 | bytes 3000000 | tf_op jit(solution)/shard_map/own_terms/pallas_call | solution.py:440
  45.8 1.2 collective-permute-start.8
  47.0 3.2 %collective-permute-start.10 = (bf16[64,128]{1,0:T(8,128)(2,1)S(1)}, bf16[64,128]{1,0:T(8,128)(2,1)S(1)}, u32[]{:S(2)}, u32[]{:S(2)}) collective-permute-start(bf16[64,128]{1,0:T(8,128)(2,1)S(1)} %get-tuple-element.30), channel_id=1, source_target_pairs={{0,32},{16,48},{32,64},{48,80},{64,96},{80,112},{96,0},{112,16},{1... | collective-permute-start | bytes 49160 | tf_op jit(solution)/shard_map/ppermute | solution.py:415
  50.3 3.1 %collective-permute-start.11 = (bf16[64,128]{1,0:T(8,128)(2,1)S(1)}, bf16[64,128]{1,0:T(8,128)(2,1)S(1)}, u32[]{:S(2)}, u32[]{:S(2)}) collective-permute-start(bf16[64,128]{1,0:T(8,128)(2,1)S(1)} %get-tuple-element.32), channel_id=1, source_target_pairs={{0,64},{16,80},{32,96},{48,112},{64,0},{80,16},{96,32},{112,48},{1... | collective-permute-start | bytes 49160 | tf_op jit(solution)/shard_map/ppermute | solution.py:415
  53.4 0.5 collective-permute-start.12
  53.9 3.9 %collective-permute-start.2 = (f32[3,4096]{1,0:T(4,128)S(1)}, f32[3,4096]{1,0:T(4,128)S(1)}, u32[]{:S(2)}, u32[]{:S(2)}) collective-permute-start(f32[3,4096]{1,0:T(4,128)S(1)} %copy-done.9), channel_id=1, source_target_pairs={{0,1},{1,2},{2,3},{3,4},{4,5},{5,6},{6,7},{7,8},{8,9},{9,10},{10,1... | collective-permute-start | bytes 147464 | tf_op jit(solution)/shard_map/ppermute | solution.py:378
  57.8 4.1 %collective-permute-start.3 = (f32[3,4096]{1,0:T(4,128)S(1)}, f32[3,4096]{1,0:T(4,128)S(1)}, u32[]{:S(2)}, u32[]{:S(2)}) collective-permute-start(f32[3,4096]{1,0:T(4,128)S(1)} %copy-done.9), channel_id=1, source_target_pairs={{1,0},{2,1},{3,2},{4,3},{5,4},{6,5},{7,6},{8,7},{9,8},{10,9},{11,1... | collective-permute-start | bytes 147464 | tf_op jit(solution)/shard_map/ppermute | solution.py:379
  61.9 2.7 %collective-permute-start.13 = (bf16[1216,128]{1,0:T(8,128)(2,1)S(1)}, bf16[1216,128]{1,0:T(8,128)(2,1)S(1)}, u32[]{:S(2)}, u32[]{:S(2)}) collective-permute-start(bf16[1216,128]{1,0:T(8,128)(2,1)S(1)} %get-tuple-element.17.y0), channel_id=1, source_target_pairs={{0,4},{1,5},{2,6},{3,7},{4,8},{5,9},{6,10},{7,11},{8,12},{9,13},{1... | collective-permute-start | bytes 933896 | tf_op jit(solution)/shard_map/ppermute | solution.py:436
  64.6 11.1 %halo_terms.1 = (bf16[1536,128]{1,0:T(8,128)(2,1)S(1)}, bf16[1536,128]{1,0:T(8,128)(2,1)S(1)}) custom-call(s32[8]{0:T(128)S(1)} %stack.31.meta, s32[16,40]{1,0:T(8,128)S(1)} %collective-permute-done.lists_l, s32[16,40]{1,0:T(8,128)S(1)} %collective-permute-done.1.lists_r, f32[3,4096]{1,0:T(4,128)S(1)} %collective-permute-done.2.pts_l, ...), custom_call_target="tpu_custom_call" | custom-call | flops 8999999488 | bytes 3000000 | tf_op jit(solution)/shard_map/halo_terms/pallas_call | solution.py:418
  75.8 2.3 %collective-permute-start.4 = (bf16[1536,128]{1,0:T(8,128)(2,1)S(1)}, bf16[1536,128]{1,0:T(8,128)(2,1)S(1)}, u32[]{:S(2)}, u32[]{:S(2)}) collective-permute-start(bf16[1536,128]{1,0:T(8,128)(2,1)S(1)} %get-tuple-element.13), channel_id=1, source_target_pairs={{0,1},{1,2},{2,3},{3,4},{4,5},{5,6},{6,7},{7,8},{8,9},{9,10},{10,1... | collective-permute-start | bytes 1179656 | tf_op jit(solution)/shard_map/ppermute | solution.py:433
  78.0 5.7 %collective-permute-start.5 = (bf16[1536,128]{1,0:T(8,128)(2,1)S(1)}, bf16[1536,128]{1,0:T(8,128)(2,1)S(1)}, u32[]{:S(2)}, u32[]{:S(2)}) collective-permute-start(bf16[1536,128]{1,0:T(8,128)(2,1)S(1)} %get-tuple-element.14), channel_id=1, source_target_pairs={{1,0},{2,1},{3,2},{4,3},{5,4},{6,5},{7,6},{8,7},{9,8},{10,9},{11,1... | collective-permute-start | bytes 1179656 | tf_op jit(solution)/shard_map/ppermute | solution.py:432
  83.7 3.0 %collective-permute-start.14 = (bf16[1216,128]{1,0:T(8,128)(2,1)S(1)}, bf16[1216,128]{1,0:T(8,128)(2,1)S(1)}, u32[]{:S(2)}, u32[]{:S(2)}) collective-permute-start(bf16[1216,128]{1,0:T(8,128)(2,1)S(1)} %get-tuple-element.17.y0), channel_id=1, source_target_pairs={{0,8},{1,9},{2,10},{3,11},{4,12},{5,13},{6,14},{7,15},{8,0},{9,1},... | collective-permute-start | bytes 933896 | tf_op jit(solution)/shard_map/ppermute | solution.py:436
  86.7 1.1 collective-permute-start.15
  87.8 15.6 %collective-permute-done.14.y2 = bf16[1216,128]{1,0:T(8,128)(2,1)S(1)} collective-permute-done((bf16[1216,128]{1,0:T(8,128)(2,1)S(1)}, bf16[1216,128]{1,0:T(8,128)(2,1)S(1)}, u32[]{:S(2)}, u32[]{:S(2)}) %collective-permute-start.14) | collective-permute-done | bytes 311328 | tf_op jit(solution)/shard_map/ppermute | solution.py:436
  103.4 5.3 %collective-permute-done.15.y3 = bf16[1216,128]{1,0:T(8,128)(2,1)S(1)} collective-permute-done((bf16[1216,128]{1,0:T(8,128)(2,1)S(1)}, bf16[1216,128]{1,0:T(8,128)(2,1)S(1)}, u32[]{:S(2)}, u32[]{:S(2)}) %collective-permute-start.15) | collective-permute-done | bytes 311328 | tf_op jit(solution)/shard_map/ppermute | solution.py:436
  108.7 11.0 %node_terms.1 = bf16[2,4,16,4096]{3,2,1,0:T(8,128)(2,1)S(1)} custom-call(s32[8]{0:T(128)S(1)} %stack.31.meta, s32[16,40]{1,0:T(8,128)S(1)} %concatenate.13.lists, f32[3,4096]{1,0:T(4,128)S(1)} %copy-done.9, f32[6,256,128]{2,1,0:T(8,128)S(1)} %own_terms.1.own, bf16[1536,128]{1,0:T(8,128)(2,1)S(1)} %collective-permute-done.4.halo_l, ...), custom_call_target="tpu_custom_call" | custom-call | flops 4000000000 | bytes 3000000 | tf_op jit(solution)/shard_map/node_terms/pallas_call | solution.py:455
  119.8 0.1 collective-permute-start.16
  120.0 0.1 collective-permute-start.18
  120.1 3.1 %collective-permute-start.19 = (bf16[256,128]{1,0:T(8,128)(2,1)S(1)}, bf16[256,128]{1,0:T(8,128)(2,1)S(1)}, u32[]{:S(2)}, u32[]{:S(2)}) collective-permute-start(bf16[256,128]{1,0:T(8,128)(2,1)S(1)} %pad_maximum_fusion), channel_id=1, source_target_pairs={{0,3},{1,0},{2,1},{3,2},{4,7},{5,4},{6,5},{7,6},{8,11},{9,8},{10,9... | collective-permute-start | bytes 196616 | tf_op jit(solution)/shard_map/ppermute | solution.py:438
  123.2 3.9 %collective-permute-done.17 = bf16[256,128]{1,0:T(8,128)(2,1)S(1)} collective-permute-done((bf16[256,128]{1,0:T(8,128)(2,1)S(1)}, bf16[256,128]{1,0:T(8,128)(2,1)S(1)}, u32[]{:S(2)}, u32[]{:S(2)}) %collective-permute-start.17) | collective-permute-done | bytes 65568 | tf_op jit(solution)/shard_map/ppermute | solution.py:438
  127.1 0.5 collective-permute-done.19
  127.7 0.1 fusion.8
  127.9 0.1 collective-permute-start.21
  128.0 3.1 %collective-permute-start.22 = (bf16[16,4096]{1,0:T(8,128)(2,1)S(1)}, bf16[16,4096]{1,0:T(8,128)(2,1)S(1)}, u32[]{:S(2)}, u32[]{:S(2)}) collective-permute-start(bf16[16,4096]{1,0:T(8,128)(2,1)S(1)} %get-tuple-element.22), channel_id=1, source_target_pairs={{0,96},{16,112},{32,0},{48,16},{64,32},{80,48},{96,64},{112,80},{1... | collective-permute-start | bytes 393224 | tf_op jit(solution)/shard_map/ppermute | solution.py:494
  131.2 19.8 %top_terms.1 = f32[16,4096]{1,0:T(8,128)S(1)} custom-call(s32[8]{0:T(128)S(1)} %stack.31.meta, s32[16,40]{1,0:T(8,128)S(1)} %concatenate.13.lists, f32[3,4096]{1,0:T(4,128)S(1)} %copy-done.9, bf16[1024,128]{1,0:T(8,128)(2,1)S(1)} %constant_dynamic-update-slice_fusion.5.tops), custom_call_target="tpu_custom_call" | custom-call | flops 8000000000 | bytes 3000000 | tf_op jit(solution)/shard_map/top_terms/pallas_call | solution.py:473
  151.0 0.8 fusion.4
  (52 shorter events, 0.5 us)
Async XLA Ops:
  6.0 58.6 %collective-permute-start = (s32[16,40]{1,0:T(8,128)S(1)}, s32[16,40]{1,0:T(8,128)S(1)}, u32[]{:S(2)}, u32[]{:S(2)}) collective-permute-start(s32[16,40]{1,0:T(8,128)S(1)} %concatenate.13.lists), channel_id=1, source_target_pairs={{0,1},{1,2},{2,3},{3,4},{4,5},{5,6},{6,7},{7,8},{8,9},{9,10},{10,1... | collective-permute-start | bytes 7688 | tf_op jit(solution)/shard_map/ppermute | solution.py:380
  9.8 54.8 %collective-permute-start.1 = (s32[16,40]{1,0:T(8,128)S(1)}, s32[16,40]{1,0:T(8,128)S(1)}, u32[]{:S(2)}, u32[]{:S(2)}) collective-permute-start(s32[16,40]{1,0:T(8,128)S(1)} %concatenate.13.lists), channel_id=1, source_target_pairs={{1,0},{2,1},{3,2},{4,3},{5,4},{6,5},{7,6},{8,7},{9,8},{10,9},{11,1... | collective-permute-start | bytes 7688 | tf_op jit(solution)/shard_map/ppermute | solution.py:381
  14.1 1.6 %copy-start = (bf16[8,256,512]{2,1,0:T(8,128)(2,1)S(1)}, bf16[8,256,512]{2,1,0:T(8,128)(2,1)}, u32[]{:S(2)}) copy-start(bf16[8,256,512]{2,1,0:T(8,128)(2,1)} %proj.1) | copy-start | bytes 6291460
  15.7 1.2 copy-start.1
  16.9 1.2 copy-start.2
  18.1 0.9 copy-start.3
  19.0 0.8 copy-start.4
  19.9 0.7 copy-start.5
  20.6 0.7 copy-start.6
  21.3 0.7 copy-start.7
  22.0 0.7 copy-start.8
  22.6 17.1 %copy-start.9 = (f32[3,4096]{1,0:T(4,128)S(1)}, f32[3,4096]{1,0:T(4,128)}, u32[]{:S(2)}) copy-start(f32[3,4096]{1,0:T(4,128)} %pts.7) | copy-start | bytes 147460
  36.3 10.7 %collective-permute-start.6 = (bf16[288,128]{1,0:T(8,128)(2,1)S(1)}, bf16[288,128]{1,0:T(8,128)(2,1)S(1)}, u32[]{:S(2)}, u32[]{:S(2)}) collective-permute-start(bf16[288,128]{1,0:T(8,128)(2,1)S(1)} %get-tuple-element.15), channel_id=1, source_target_pairs={{0,1},{1,2},{2,3},{3,0},{4,5},{5,6},{6,7},{7,4},{8,9},{9,10},{10,1... | collective-permute-start | bytes 221192 | tf_op jit(solution)/shard_map/ppermute | solution.py:412
  36.4 13.8 %collective-permute-start.7 = (bf16[288,128]{1,0:T(8,128)(2,1)S(1)}, bf16[288,128]{1,0:T(8,128)(2,1)S(1)}, u32[]{:S(2)}, u32[]{:S(2)}) collective-permute-start(bf16[288,128]{1,0:T(8,128)(2,1)S(1)} %get-tuple-element.15), channel_id=1, source_target_pairs={{0,2},{1,3},{2,0},{3,1},{4,6},{5,7},{6,4},{7,5},{8,10},{9,11},{10,... | collective-permute-start | bytes 221192 | tf_op jit(solution)/shard_map/ppermute | solution.py:412
  39.8 6.0 %collective-permute-start.9 = (bf16[4,64,128]{2,1,0:T(8,128)(2,1)S(1)}, bf16[4,64,128]{2,1,0:T(8,128)(2,1)S(1)}, u32[]{:S(2)}, u32[]{:S(2)}) collective-permute-start(bf16[4,64,128]{2,1,0:T(8,128)(2,1)S(1)} %slice_bitcast_fusion.6), channel_id=1, source_target_pairs={{0,16},{16,0},{32,48},{48,32},{64,80},{80,64},{96,112},{112,96},{1... | collective-permute-start | bytes 196616 | tf_op jit(solution)/shard_map/ppermute | solution.py:411
  45.8 7.6 %collective-permute-start.8 = (bf16[288,128]{1,0:T(8,128)(2,1)S(1)}, bf16[288,128]{1,0:T(8,128)(2,1)S(1)}, u32[]{:S(2)}, u32[]{:S(2)}) collective-permute-start(bf16[288,128]{1,0:T(8,128)(2,1)S(1)} %get-tuple-element.15), channel_id=1, source_target_pairs={{0,3},{1,0},{2,1},{3,2},{4,7},{5,4},{6,5},{7,6},{8,11},{9,8},{10,9... | collective-permute-start | bytes 221192 | tf_op jit(solution)/shard_map/ppermute | solution.py:412
  47.0 6.9 %collective-permute-start.10 = (bf16[64,128]{1,0:T(8,128)(2,1)S(1)}, bf16[64,128]{1,0:T(8,128)(2,1)S(1)}, u32[]{:S(2)}, u32[]{:S(2)}) collective-permute-start(bf16[64,128]{1,0:T(8,128)(2,1)S(1)} %get-tuple-element.30), channel_id=1, source_target_pairs={{0,32},{16,48},{32,64},{48,80},{64,96},{80,112},{96,0},{112,16},{1... | collective-permute-start | bytes 49160 | tf_op jit(solution)/shard_map/ppermute | solution.py:415
  50.3 7.6 %collective-permute-start.11 = (bf16[64,128]{1,0:T(8,128)(2,1)S(1)}, bf16[64,128]{1,0:T(8,128)(2,1)S(1)}, u32[]{:S(2)}, u32[]{:S(2)}) collective-permute-start(bf16[64,128]{1,0:T(8,128)(2,1)S(1)} %get-tuple-element.32), channel_id=1, source_target_pairs={{0,64},{16,80},{32,96},{48,112},{64,0},{80,16},{96,32},{112,48},{1... | collective-permute-start | bytes 49160 | tf_op jit(solution)/shard_map/ppermute | solution.py:415
  53.4 8.5 %collective-permute-start.12 = (bf16[64,128]{1,0:T(8,128)(2,1)S(1)}, bf16[64,128]{1,0:T(8,128)(2,1)S(1)}, u32[]{:S(2)}, u32[]{:S(2)}) collective-permute-start(bf16[64,128]{1,0:T(8,128)(2,1)S(1)} %get-tuple-element.31), channel_id=1, source_target_pairs={{0,96},{16,112},{32,0},{48,16},{64,32},{80,48},{96,64},{112,80},{1... | collective-permute-start | bytes 49160 | tf_op jit(solution)/shard_map/ppermute | solution.py:415
  53.9 10.7 %collective-permute-start.2 = (f32[3,4096]{1,0:T(4,128)S(1)}, f32[3,4096]{1,0:T(4,128)S(1)}, u32[]{:S(2)}, u32[]{:S(2)}) collective-permute-start(f32[3,4096]{1,0:T(4,128)S(1)} %copy-done.9), channel_id=1, source_target_pairs={{0,1},{1,2},{2,3},{3,4},{4,5},{5,6},{6,7},{7,8},{8,9},{9,10},{10,1... | collective-permute-start | bytes 147464 | tf_op jit(solution)/shard_map/ppermute | solution.py:378
  57.8 6.8 %collective-permute-start.3 = (f32[3,4096]{1,0:T(4,128)S(1)}, f32[3,4096]{1,0:T(4,128)S(1)}, u32[]{:S(2)}, u32[]{:S(2)}) collective-permute-start(f32[3,4096]{1,0:T(4,128)S(1)} %copy-done.9), channel_id=1, source_target_pairs={{1,0},{2,1},{3,2},{4,3},{5,4},{6,5},{7,6},{8,7},{9,8},{10,9},{11,1... | collective-permute-start | bytes 147464 | tf_op jit(solution)/shard_map/ppermute | solution.py:379
  61.9 25.9 %collective-permute-start.13 = (bf16[1216,128]{1,0:T(8,128)(2,1)S(1)}, bf16[1216,128]{1,0:T(8,128)(2,1)S(1)}, u32[]{:S(2)}, u32[]{:S(2)}) collective-permute-start(bf16[1216,128]{1,0:T(8,128)(2,1)S(1)} %get-tuple-element.17.y0), channel_id=1, source_target_pairs={{0,4},{1,5},{2,6},{3,7},{4,8},{5,9},{6,10},{7,11},{8,12},{9,13},{1... | collective-permute-start | bytes 933896 | tf_op jit(solution)/shard_map/ppermute | solution.py:436
  75.8 33.0 %collective-permute-start.4 = (bf16[1536,128]{1,0:T(8,128)(2,1)S(1)}, bf16[1536,128]{1,0:T(8,128)(2,1)S(1)}, u32[]{:S(2)}, u32[]{:S(2)}) collective-permute-start(bf16[1536,128]{1,0:T(8,128)(2,1)S(1)} %get-tuple-element.13), channel_id=1, source_target_pairs={{0,1},{1,2},{2,3},{3,4},{4,5},{5,6},{6,7},{7,8},{8,9},{9,10},{10,1... | collective-permute-start | bytes 1179656 | tf_op jit(solution)/shard_map/ppermute | solution.py:433
  78.0 30.7 %collective-permute-start.5 = (bf16[1536,128]{1,0:T(8,128)(2,1)S(1)}, bf16[1536,128]{1,0:T(8,128)(2,1)S(1)}, u32[]{:S(2)}, u32[]{:S(2)}) collective-permute-start(bf16[1536,128]{1,0:T(8,128)(2,1)S(1)} %get-tuple-element.14), channel_id=1, source_target_pairs={{1,0},{2,1},{3,2},{4,3},{5,4},{6,5},{7,6},{8,7},{9,8},{10,9},{11,1... | collective-permute-start | bytes 1179656 | tf_op jit(solution)/shard_map/ppermute | solution.py:432
  83.7 19.7 %collective-permute-start.14 = (bf16[1216,128]{1,0:T(8,128)(2,1)S(1)}, bf16[1216,128]{1,0:T(8,128)(2,1)S(1)}, u32[]{:S(2)}, u32[]{:S(2)}) collective-permute-start(bf16[1216,128]{1,0:T(8,128)(2,1)S(1)} %get-tuple-element.17.y0), channel_id=1, source_target_pairs={{0,8},{1,9},{2,10},{3,11},{4,12},{5,13},{6,14},{7,15},{8,0},{9,1},... | collective-permute-start | bytes 933896 | tf_op jit(solution)/shard_map/ppermute | solution.py:436
  86.7 22.0 %collective-permute-start.15 = (bf16[1216,128]{1,0:T(8,128)(2,1)S(1)}, bf16[1216,128]{1,0:T(8,128)(2,1)S(1)}, u32[]{:S(2)}, u32[]{:S(2)}) collective-permute-start(bf16[1216,128]{1,0:T(8,128)(2,1)S(1)} %get-tuple-element.17.y0), channel_id=1, source_target_pairs={{0,12},{1,13},{2,14},{3,15},{4,0},{5,1},{6,2},{7,3},{8,4},{9,5},{1... | collective-permute-start | bytes 933896 | tf_op jit(solution)/shard_map/ppermute | solution.py:436
  119.8 7.9 %collective-permute-start.16 = (bf16[4,16,4096]{2,1,0:T(8,128)(2,1)S(1)}, bf16[4,16,4096]{2,1,0:T(8,128)(2,1)S(1)}, u32[]{:S(2)}, u32[]{:S(2)}) collective-permute-start(bf16[4,16,4096]{2,1,0:T(8,128)(2,1)S(1)} %slice_bitcast_fusion), channel_id=1, source_target_pairs={{0,16},{16,0},{32,48},{48,32},{64,80},{80,64},{96,112},{112,96},{1... | collective-permute-start | bytes 1572872 | tf_op jit(solution)/shard_map/ppermute | solution.py:491
  119.9 7.2 %collective-permute-start.17 = (bf16[256,128]{1,0:T(8,128)(2,1)S(1)}, bf16[256,128]{1,0:T(8,128)(2,1)S(1)}, u32[]{:S(2)}, u32[]{:S(2)}) collective-permute-start(bf16[256,128]{1,0:T(8,128)(2,1)S(1)} %pad_maximum_fusion), channel_id=1, source_target_pairs={{0,1},{1,2},{2,3},{3,0},{4,5},{5,6},{6,7},{7,4},{8,9},{9,10},{10,1... | collective-permute-start | bytes 196616 | tf_op jit(solution)/shard_map/ppermute | solution.py:438
  120.0 7.1 %collective-permute-start.18 = (bf16[256,128]{1,0:T(8,128)(2,1)S(1)}, bf16[256,128]{1,0:T(8,128)(2,1)S(1)}, u32[]{:S(2)}, u32[]{:S(2)}) collective-permute-start(bf16[256,128]{1,0:T(8,128)(2,1)S(1)} %pad_maximum_fusion), channel_id=1, source_target_pairs={{0,2},{1,3},{2,0},{3,1},{4,6},{5,7},{6,4},{7,5},{8,10},{9,11},{10,... | collective-permute-start | bytes 196616 | tf_op jit(solution)/shard_map/ppermute | solution.py:438
  120.1 7.6 %collective-permute-start.19 = (bf16[256,128]{1,0:T(8,128)(2,1)S(1)}, bf16[256,128]{1,0:T(8,128)(2,1)S(1)}, u32[]{:S(2)}, u32[]{:S(2)}) collective-permute-start(bf16[256,128]{1,0:T(8,128)(2,1)S(1)} %pad_maximum_fusion), channel_id=1, source_target_pairs={{0,3},{1,0},{2,1},{3,2},{4,7},{5,4},{6,5},{7,6},{8,11},{9,8},{10,9... | collective-permute-start | bytes 196616 | tf_op jit(solution)/shard_map/ppermute | solution.py:438
  127.9 23.1 %collective-permute-start.20 = (bf16[16,4096]{1,0:T(8,128)(2,1)S(1)}, bf16[16,4096]{1,0:T(8,128)(2,1)S(1)}, u32[]{:S(2)}, u32[]{:S(2)}) collective-permute-start(bf16[16,4096]{1,0:T(8,128)(2,1)S(1)} %get-tuple-element.21), channel_id=1, source_target_pairs={{0,32},{16,48},{32,64},{48,80},{64,96},{80,112},{96,0},{112,16},{1... | collective-permute-start | bytes 393224 | tf_op jit(solution)/shard_map/ppermute | solution.py:494
  127.9 23.0 %collective-permute-start.21 = (bf16[16,4096]{1,0:T(8,128)(2,1)S(1)}, bf16[16,4096]{1,0:T(8,128)(2,1)S(1)}, u32[]{:S(2)}, u32[]{:S(2)}) collective-permute-start(bf16[16,4096]{1,0:T(8,128)(2,1)S(1)} %get-tuple-element.23), channel_id=1, source_target_pairs={{0,64},{16,80},{32,96},{48,112},{64,0},{80,16},{96,32},{112,48},{1... | collective-permute-start | bytes 393224 | tf_op jit(solution)/shard_map/ppermute | solution.py:494
  128.0 22.9 %collective-permute-start.22 = (bf16[16,4096]{1,0:T(8,128)(2,1)S(1)}, bf16[16,4096]{1,0:T(8,128)(2,1)S(1)}, u32[]{:S(2)}, u32[]{:S(2)}) collective-permute-start(bf16[16,4096]{1,0:T(8,128)(2,1)S(1)} %get-tuple-element.22), channel_id=1, source_target_pairs={{0,96},{16,112},{32,0},{48,16},{64,32},{80,48},{96,64},{112,80},{1... | collective-permute-start | bytes 393224 | tf_op jit(solution)/shard_map/ppermute | solution.py:494
